TPU v7x, 32 devices: a whole 2x2x4 slice. The times are simulated.
32 devices in a mesh: box: 8 (over z, x), sub: 4 (over y, core).
Axes of the slice: x: 2, y: 2, z: 4, core: 2. Of those that a mesh axis runs over, the one named last changes fastest.
Arguments:
- leaves: bfloat16 [1024, 16, 256], P(('box', 'sub')), may hold values from -6 to 6
- local_src: int32 [1024, 8], P(('box', 'sub')), may hold values from 0 to 31
- local_cls: int32 [1024, 8], P(('box', 'sub')), may hold values from 0 to 11
- send_box: int32 [32, 8, 2], P(('box', 'sub')), may hold values from 0 to 31
- recv_tgt: int32 [32, 8, 2], P(('box', 'sub')), may hold values from 0 to 31
- recv_cls: int32 [32, 8, 2], P(('box', 'sub')), may hold values from 0 to 11
- recv_live: int32 [32, 8, 2], P(('box', 'sub')), may hold values from 0 to 1, as said below
- translation: bfloat16 [12, 256, 256], replicated, may hold values from -0.125 to 0.125
- up_maps: bfloat16 [4, 8, 256, 256], P('sub'), may hold values from -0.09375 to 0.09375
- down_maps: bfloat16 [4, 8, 256, 256], P('sub'), may hold values from -0.375 to 0.375
- coupling: float32 [8, 8], replicated, may hold values from -2 to 2
Outputs:
- pressure_adjoint: bfloat16 [1024, 16, 256], P(('box', 'sub'))
Inputs may be any that keep to these rules, and one draw needn't show every extreme that they name: `recv_live`: among the devices with one index along sub, one drawn from the seed has every received slot live.
All inputs are finite; a program needn't handle non-finite values.
Results may differ from a plain program's by a relative error of at most 0.01.
Values may be sent and summed in bfloat16 or wider, within the bound.
A program may use at most 64 MiB of HBM per device.

v0:
```python
import jax
import jax.numpy as jnp
from jax import lax
from jax.sharding import PartitionSpec as P


def local(
    leaves,
    local_src,
    local_cls,
    send_box,
    recv_tgt,
    recv_cls,
    recv_live,
    translation,
    up_maps,
    down_maps,
    coupling,
):
    box_count = leaves.shape[0]
    width = leaves.shape[1] * leaves.shape[2]
    classes_total = translation.shape[0]
    outgoing = leaves[send_box[0]]
    arrived = lax.all_to_all(outgoing, "box", split_axis=0, concat_axis=0, tiled=True)
    near_rows = leaves[local_src]
    stacked = jnp.concatenate(
        [arrived.reshape(-1, width), near_rows.reshape(-1, width)], axis=0
    ).astype(jnp.float32)
    weights = jnp.concatenate(
        [recv_live[0].reshape(-1), jnp.ones((local_src.size,), jnp.int32)]
    ).astype(jnp.float32)
    own_ids = jnp.arange(box_count, dtype=jnp.int32)[:, None]
    segment_ids = jnp.concatenate(
        [
            (recv_cls[0] * box_count + recv_tgt[0]).reshape(-1),
            (local_cls * box_count + own_ids).reshape(-1),
        ]
    )
    summed = jax.ops.segment_sum(
        stacked * weights[:, None], segment_ids, num_segments=classes_total * box_count
    )
    grouped = summed.astype(jnp.bfloat16).reshape(
        classes_total, box_count, leaves.shape[1], leaves.shape[2]
    )
    near_field = jnp.einsum(
        "cbsp,cqp->bsq", grouped, translation, preferred_element_type=jnp.float32
    )
    child_sum = jnp.sum(
        leaves.astype(jnp.float32).reshape(box_count // 8, 8, leaves.shape[1], leaves.shape[2]),
        axis=0,
    ).astype(jnp.bfloat16)
    partial_value = jnp.einsum(
        "csp,cqp->sq", child_sum, up_maps[0], preferred_element_type=jnp.float32
    )
    box_index = lax.axis_index("box")
    coupling_row = lax.dynamic_index_in_dim(coupling, box_index, 0, False)
    top_sum = lax.psum(partial_value, "sub")
    far_sum = jnp.einsum(
        "r,rsp->sp",
        coupling_row,
        lax.all_gather(top_sum[None], "box", axis=0, tiled=True),
        precision=lax.Precision.HIGHEST,
    )
    far_field = jnp.einsum(
        "sp,cqp->csq",
        far_sum.astype(jnp.bfloat16),
        down_maps[0],
        preferred_element_type=jnp.float32,
    )
    total = (
        near_field.reshape(box_count // 8, 8, leaves.shape[1], leaves.shape[2]) + far_field[None]
    )
    return total.reshape(leaves.shape).astype(jnp.bfloat16)


def solution(mesh):
    in_specs = (
        P(("box", "sub"), None, None),
        P(("box", "sub"), None),
        P(("box", "sub"), None),
        P(("box", "sub"), None, None),
        P(("box", "sub"), None, None),
        P(("box", "sub"), None, None),
        P(("box", "sub"), None, None),
        P(),
        P("sub", None, None, None),
        P("sub", None, None, None),
        P(),
    )
    out_specs = P(("box", "sub"), None, None)
    return jax.shard_map(local, mesh=mesh, in_specs=in_specs, out_specs=out_specs, check_vma=False)
```

profile of v0, /device:TPU:0, one launch (start us, length us, event | category | flops | bytes accessed | tf_op | source)
XLA Modules:
  0.0 82.3 jit_solution(16795540948153272847)
XLA Ops:
  0.0 0.0 copy-start
  0.0 0.8 compare_select_fusion.1
  0.8 0.1 copy.29
  0.9 0.1 reshape.66
  1.0 2.2 %gather_fusion = bf16[16,16,256]{2,1,0:T(8,128)(2,1)} fusion(bf16[32,16,256]{2,1,0:T(8,128)(2,1)} %param.11, s32[1024]{0:T(1024)S(1)} %pad_clamp_fusion.1), kind=kCustom, calls=%fused_computation | custom fusion | bytes 262208 | tf_op jit(solution)/shard_map/gather | solution.py:23
  3.1 7.3 %all-to-all-start = ((bf16[8,2,16,256]{3,2,1,0:T(8,128)(2,1)}), bf16[8,2,16,256]{3,2,1,0:T(8,128)(2,1)S(1)}, u32[]{:S(2)}, u32[]{:S(2)}) async-start(bf16[8,2,16,256]{3,2,1,0:T(8,128)(2,1)} %bitcast.1), calls=%async_computation | async-start | bytes 262144 | tf_op jit(solution)/shard_map/all_to_all | solution.py:24
  10.4 0.7 iota_add_fusion
  11.1 0.1 copy.28
  11.2 0.1 reshape.58
  11.3 0.7 multiply_add_fusion
  12.0 0.1 copy.27
  12.0 0.1 add.47
  12.1 0.8 copy.31
  12.9 0.1 reshape_squeeze.3
  13.0 0.7 compare_select_fusion
  13.7 0.1 copy.30
  13.7 0.1 reshape.74
  13.8 3.1 %gather_fusion.1 = bf16[256,16,256]{2,1,0:T(8,128)(2,1)} fusion(bf16[32,16,256]{2,1,0:T(8,128)(2,1)} %param.11, s32[1024]{0:T(1024)S(1)} %pad_clamp_fusion), kind=kCustom, calls=%fused_computation.1 | custom fusion | bytes 4195328 | tf_op jit(solution)/shard_map/gather | solution.py:25
  16.9 4.0 %copy.38 = bf16[32,8,16,256]{3,1,2,0:T(8,128)(2,1)} copy(bf16[32,8,16,256]{3,2,1,0:T(8,128)(2,1)} %bitcast.56) | data formatting | bytes 4194304
  20.9 1.6 %convolution_bitcast_fusion.1 = f32[1,16,256]{2,1,0:T(8,128)S(1)} fusion(bf16[8,16,256]{2,1,0:T(8,128)(2,1)S(1)} %reduce, bf16[1,8,256,256]{3,2,1,0:T(8,128)(2,1)} %param.19), kind=kOutput, calls=%fused_computation.15 | convolution fusion | flops 16777216 | bytes 1130496 | tf_op jit(solution)/shard_map/csp,cqp->sq/dot_general | solution.py:52
  22.5 10.7 %psum.7 = f32[1,16,256]{2,1,0:T(8,128)S(1)} all-reduce(f32[1,16,256]{2,1,0:T(8,128)S(1)} %convolution_bitcast_fusion.1), channel_id=1, replica_groups=mesh['box'=8,'sub'=4] {'sub'}, use_global_device_ids=true, to_apply=%region_2.3 | all-reduce | flops 4096 | bytes 32768 | tf_op jit(solution)/shard_map/psum | solution.py:57
  33.2 30.8 %all_gather.3 = f32[8,16,256]{2,1,0:T(8,128)S(1)} all-gather(f32[1,16,256]{2,1,0:T(8,128)S(1)} %psum.7), channel_id=1, replica_groups=mesh['box'=8,'sub'=4] {'box'}, dimensions={0}, use_global_device_ids=true | all-gather | bytes 147456 | tf_op jit(solution)/shard_map/all_gather | solution.py:61
  64.0 0.1 pad_add_fusion
  64.0 1.0 %fusion.14 = bf16[1,16,256]{2,0,1:T(2,128)(2,1)S(1)} fusion(f32[8,16,256]{2,1,0:T(8,128)S(1)} %all_gather.3, f32[8,8]{1,0:T(8,128)} %param.21, s32[]{:T(128)S(6)} %select_n.19), kind=kOutput, calls=%fused_computation.20 | convolution fusion | flops 393216 | bytes 139780 | tf_op jit(solution)/shard_map/r,rsp->sp/dot_general | solution.py:58
  65.1 0.4 convolution_bitcast_fusion
  65.4 0.0 all-to-all-done
  65.4 0.1 copy.37
  65.5 10.7 %scatter_custom_fusion = f32[384,4096]{1,0:T(8,128)} fusion(s32[272]{0:T(512)S(1)} %get-tuple-element.5, f32[]{:T(128)} %constant.7.clone.1, bf16[256,4096]{1,0:T(8,128)(2,1)} %bitcast.55, bf16[]{:T(256)} %constant.31, bf16[16,4096]{1,0:T(8,128)(2,1)S(1)} %bitcast.58, f32[272]{0:T(512)S(1)} %get-tuple-element.6), kind=kCustom, calls=%fused_computation.3 | custom fusion | flops 6684672 | bytes 8521734 | tf_op jit(solution)/shard_map/scatter-add | solution.py:39
  76.2 3.2 %convert_element_type.24 = bf16[384,4096]{1,0:T(8,128)(2,1)S(1)} convert(f32[384,4096]{1,0:T(8,128)} %scatter_custom_fusion) | non-fusion elementwise | flops 1572864 | bytes 9437184 | tf_op jit(solution)/shard_map/convert_element_type | solution.py:42
  79.5 1.0 %copy.39 = bf16[48,8,16,256]{3,2,1,0:T(8,128)(2,1)S(1)} copy(bf16[48,8,16,256]{3,1,2,0:T(8,128)(2,1)S(1)} %bitcast.54) | data formatting | bytes 6291456
  80.5 1.0 %fusion.3 = f32[4,8,16,256,1]{3,2,0,1,4:T(8,128)S(1)} fusion(bf16[4,8,16,12,256]{4,2,1,0,3:T(8,128)(2,1)S(1)} %bitcast.57, bf16[12,256,256]{2,1,0:T(8,128)(2,1)S(1)} %copy-done), kind=kOutput, calls=%fused_computation.6 | convolution fusion | flops 805306368 | bytes 5242880 | tf_op jit(solution)/shard_map/cbsp,cqp->bsq/dot_general | solution.py:45
  81.5 0.8 fusion.13
  (8 shorter events, 0.1 us)
Async XLA Ops:
  0.0 80.5 %copy-start = (bf16[12,256,256]{2,1,0:T(8,128)(2,1)S(1)}, bf16[12,256,256]{2,1,0:T(8,128)(2,1)}, u32[]{:S(2)}) copy-start(bf16[12,256,256]{2,1,0:T(8,128)(2,1)} %param.18) | copy-start | bytes 4718596
  3.1 62.3 %all-to-all-start = ((bf16[8,2,16,256]{3,2,1,0:T(8,128)(2,1)}), bf16[8,2,16,256]{3,2,1,0:T(8,128)(2,1)S(1)}, u32[]{:S(2)}, u32[]{:S(2)}) async-start(bf16[8,2,16,256]{3,2,1,0:T(8,128)(2,1)} %bitcast.1), calls=%async_computation | async-start | bytes 262144 | tf_op jit(solution)/shard_map/all_to_all | solution.py:24
  16.9 4.0 %copy-start.1 = (bf16[32,16,256]{2,1,0:T(8,128)(2,1)S(1)}, bf16[32,16,256]{2,1,0:T(8,128)(2,1)}, u32[]{:S(2)}) copy-start(bf16[32,16,256]{2,1,0:T(8,128)(2,1)} %param.11) | copy-start | bytes 786436
  16.9 48.1 %copy-start.2 = (bf16[1,8,256,256]{3,2,1,0:T(8,128)(2,1)S(1)}, bf16[1,8,256,256]{3,2,1,0:T(8,128)(2,1)}, u32[]{:S(2)}) copy-start(bf16[1,8,256,256]{3,2,1,0:T(8,128)(2,1)} %param.20) | copy-start | bytes 3145732
where the time goes:
time: 82.8 us; the launch traced here: 82.3 us
  blocking collectives  41.5 us (50%)
  other arithmetic  17.8 us (21%)
  local copies, waits for them, and re-layouts  11.8 us (14%)
  starting transfers between devices  7.25 us (9%)
  matrix products  3.96 us (5%)
    all_gather x1, blocking collectives, local(): lax.all_gather(top_sum[None], 'box', axis=0, tiled=True)  30.8 us
    scatter-add x1, other arithmetic, local(): jax.ops.segment_sum(stacked * weights[:, None], segment_ids, num_segments...  10.7 us
    psum x1, blocking collectives, local(): top_sum = lax.psum(partial_value, 'sub')  10.7 us
    all_to_all x1, starting transfers between devices, local(): lax.all_to_all(outgoing, 'box', split_axis=0, concat_axis=0, tiled=True)  7.25 us
    unnamed x10, local copies, waits for them, and re-layouts  5.83 us
    convert_element_type x1, other arithmetic, local(): summed.astype(jnp.bfloat16)  3.22 us
    gather x1, local copies, waits for them, and re-layouts, local(): near_rows = leaves[local_src]  3.06 us
    gather x1, local copies, waits for them, and re-layouts, local(): outgoing = leaves[send_box[0]]  2.16 us
  transfers between devices with their start and end apart: 1, of which 0 were waited for; matrix products, arithmetic and copies ran while one was open for 16% of the time, Pallas kernels for 0%

commit v1 on v0

v1 whole, which is shorter than its diff:
```python
import functools

import jax
import jax.numpy as jnp
from jax import lax
from jax.experimental import pallas as pl
from jax.experimental.pallas import tpu as pltpu
from jax.sharding import PartitionSpec as P

MESH = pl.DeviceIdType.MESH
F32 = jnp.float32
BF16 = jnp.bfloat16


def dot_nt(a, b):
    return lax.dot_general(a, b, (((1,), (1,)), ((), ())), preferred_element_type=F32)


def swap_matrix(outer, inner):
    size = outer * inner
    row = lax.broadcasted_iota(jnp.int32, (size, 1), 0)
    source = (row % inner) * outer + row // inner
    column = lax.broadcasted_iota(jnp.int32, (size, size), 1)
    return jnp.where(column == source, 1.0, 0.0).astype(BF16)


def kernel(
    nb,
    ns,
    leaves_hbm,
    src_ref,
    cls_ref,
    send_box,
    recv_tgt,
    recv_cls,
    recv_live,
    trans_hbm,
    up_hbm,
    down_hbm,
    coupling,
    out_ref,
    leaves,
    trans,
    up,
    down,
    outgoing,
    arrived,
    part_out,
    parts,
    top_out,
    tops,
    mixed,
    counts,
    grouped,
    near,
    load_sem,
    slot_send,
    slot_recv,
    part_send,
    part_recv,
    top_send,
    top_recv,
):
    box = lax.axis_index("box")
    sub = lax.axis_index("sub")
    boxes, rhs, width = leaves.shape
    cap = outgoing.shape[1]
    classes = trans.shape[0]
    children = up.shape[0]
    slots = nb * cap
    depth = boxes + slots

    def box_peer(d):
        return (lax.rem(box + d, nb), sub)

    def sub_peer(d):
        return (box, lax.rem(sub + d, ns))

    def over(count, body):
        if count <= 16:
            for d in range(1, count):
                body(d)
        else:
            pl.loop(1, count)(body)

    barrier = pltpu.get_barrier_semaphore()
    over(ns, lambda d: pl.semaphore_signal(barrier, inc=1, device_id=sub_peer(d), device_id_type=MESH))
    over(nb, lambda d: pl.semaphore_signal(barrier, inc=1, device_id=box_peer(d), device_id_type=MESH))

    loads = [
        pltpu.make_async_copy(leaves_hbm, leaves, load_sem.at[0]),
        pltpu.make_async_copy(up_hbm.at[0], up, load_sem.at[1]),
        pltpu.make_async_copy(trans_hbm, trans, load_sem.at[2]),
        pltpu.make_async_copy(down_hbm.at[0], down, load_sem.at[3]),
    ]
    for load in loads:
        load.start()

    lane = lax.broadcasted_iota(jnp.int32, (1, depth), 1)
    slot_code = jnp.full((1, depth), -1, jnp.int32)

    def add_slot(d, c, code):
        k = lax.rem(box - d + nb, nb)
        value = recv_cls[0, k, c] * boxes + recv_tgt[0, k, c]
        value = jnp.where(recv_live[0, k, c] != 0, value, -1)
        return jnp.where(lane == boxes + d * cap + c, value, code)

    if nb <= 16:
        for d in range(nb):
            for c in range(cap):
                slot_code = add_slot(d, c, slot_code)
    else:
        def add_peer(d, code):
            for c in range(cap):
                code = add_slot(d, c, code)
            return code

        slot_code = lax.fori_loop(0, nb, add_peer, slot_code)
    own_code = cls_ref[...] * depth + src_ref[...]
    target = lax.broadcasted_iota(jnp.int32, (boxes, depth), 0)
    for q in range(classes):
        total = jnp.where(slot_code == q * boxes + target, 1.0, 0.0)
        for n in range(own_code.shape[1]):
            total += jnp.where(own_code[:, n : n + 1] == q * depth + lane, 1.0, 0.0)
        counts[q * boxes : (q + 1) * boxes, :] = total.astype(BF16)

    loads[0].wait()

    if nb <= 16:
        for d in range(nb):
            for c in range(cap):
                k = lax.rem(box + d, nb)
                outgoing[d, c] = leaves[send_box[0, k, c]]
    else:
        @pl.loop(0, nb)
        def _(d):
            for c in range(cap):
                outgoing[d, c] = leaves[send_box[0, lax.rem(box + d, nb), c]]

    for c in range(cap):
        arrived[0, c] = outgoing[0, c]

    child = leaves[0:children].astype(F32)
    for g in range(1, boxes // children):
        child += leaves[g * children : (g + 1) * children].astype(F32)
    child = child.astype(BF16)

    loads[1].wait()
    part = dot_nt(child[0], up[0])
    for m in range(1, children):
        part += dot_nt(child[m], up[m])
    part_out[...] = part.astype(BF16)

    pl.semaphore_wait(barrier, nb + ns - 2)

    def part_copy(d):
        return pltpu.make_async_remote_copy(
            src_ref=part_out,
            dst_ref=parts.at[d],
            send_sem=part_send.at[d],
            recv_sem=part_recv.at[d],
            device_id=sub_peer(d),
            device_id_type=MESH,
        )

    def slot_copy(d):
        return pltpu.make_async_remote_copy(
            src_ref=outgoing.at[d],
            dst_ref=arrived.at[d],
            send_sem=slot_send.at[d],
            recv_sem=slot_recv.at[d],
            device_id=box_peer(d),
            device_id_type=MESH,
        )

    def top_copy(d):
        return pltpu.make_async_remote_copy(
            src_ref=top_out,
            dst_ref=tops.at[d],
            send_sem=top_send.at[d],
            recv_sem=top_recv.at[d],
            device_id=box_peer(d),
            device_id_type=MESH,
        )

    over(ns, lambda d: part_copy(d).start())
    over(nb, lambda d: slot_copy(d).start())

    mixed[:, 0:boxes, :] = (
        jnp.dot(
            swap_matrix(rhs, boxes),
            leaves[...].reshape(boxes * rhs, width),
            preferred_element_type=F32,
        )
        .astype(BF16)
        .reshape(rhs, boxes, width)
    )

    top = part
    over(ns, lambda d: part_copy(d).wait_recv())
    for d in range(1, ns):
        top += parts[d].astype(F32)
    top_out[...] = top.astype(BF16)
    over(nb, lambda d: top_copy(d).start())

    over(nb, lambda d: slot_copy(d).wait_recv())
    group = 16
    swap_slots = swap_matrix(rhs, group)
    per_group = group // cap
    for g in range(slots // group):
        rows = arrived[g * per_group : (g + 1) * per_group].reshape(group * rhs, width)
        mixed[:, boxes + g * group : boxes + (g + 1) * group, :] = (
            jnp.dot(swap_slots, rows, preferred_element_type=F32)
            .astype(BF16)
            .reshape(rhs, group, width)
        )

    for s in range(rhs):
        held = jnp.dot(counts[...], mixed[s], preferred_element_type=F32).astype(BF16)
        grouped[:, s * boxes : (s + 1) * boxes, :] = held.reshape(classes, boxes, width)

    loads[2].wait()
    total = dot_nt(grouped[0], trans[0])
    for q in range(1, classes):
        total += dot_nt(grouped[q], trans[q])
    high = total.astype(BF16)
    low = (total - high.astype(F32)).astype(BF16)
    back = swap_matrix(boxes, rhs)
    near[...] = (
        jnp.dot(back, high, preferred_element_type=F32)
        + jnp.dot(back, low, preferred_element_type=F32)
    ).reshape(boxes, rhs, width)

    loads[3].wait()
    over(nb, lambda d: top_copy(d).wait_recv())
    far = coupling[box, box] * top
    if nb <= 16:
        for d in range(1, nb):
            far += coupling[box, lax.rem(box - d + nb, nb)] * tops[d].astype(F32)
    else:
        far = lax.fori_loop(
            1,
            nb,
            lambda d, far: far + coupling[box, lax.rem(box - d + nb, nb)] * tops[d].astype(F32),
            far,
        )
    far = far.astype(BF16)
    for m in range(children):
        field = dot_nt(far, down[m])
        for g in range(boxes // children):
            b = g * children + m
            out_ref[b] = (near[b] + field).astype(BF16)

    over(ns, lambda d: part_copy(d).wait_send())
    over(nb, lambda d: slot_copy(d).wait_send())
    over(nb, lambda d: top_copy(d).wait_send())


def local(nb, ns, *args):
    leaves, local_src, local_cls, send_box, recv_tgt, recv_cls, recv_live = args[:7]
    translation, up_maps, down_maps, coupling = args[7:]
    boxes, rhs, width = leaves.shape
    cap = send_box.shape[2]
    classes = translation.shape[0]
    depth = boxes + nb * cap
    vmem = pl.BlockSpec(memory_space=pltpu.VMEM)
    smem = pl.BlockSpec(memory_space=pltpu.SMEM)
    hbm = pl.BlockSpec(memory_space=pl.ANY)
    dma = pltpu.SemaphoreType.DMA
    return pl.pallas_call(
        functools.partial(kernel, nb, ns),
        out_shape=jax.ShapeDtypeStruct(leaves.shape, BF16),
        in_specs=[hbm, vmem, vmem, smem, smem, smem, smem, hbm, hbm, hbm, smem],
        out_specs=vmem,
        scratch_shapes=[
            pltpu.VMEM((boxes, rhs, width), BF16),
            pltpu.VMEM(translation.shape, BF16),
            pltpu.VMEM(up_maps.shape[1:], BF16),
            pltpu.VMEM(down_maps.shape[1:], BF16),
            pltpu.VMEM((nb, cap, rhs, width), BF16),
            pltpu.VMEM((nb, cap, rhs, width), BF16),
            pltpu.VMEM((rhs, width), BF16),
            pltpu.VMEM((ns, rhs, width), BF16),
            pltpu.VMEM((rhs, width), BF16),
            pltpu.VMEM((nb, rhs, width), BF16),
            pltpu.VMEM((rhs, depth, width), BF16),
            pltpu.VMEM((classes * boxes, depth), BF16),
            pltpu.VMEM((classes, rhs * boxes, width), BF16),
            pltpu.VMEM((boxes, rhs, width), F32),
            dma((4,)),
            dma((nb,)),
            dma((nb,)),
            dma((ns,)),
            dma((ns,)),
            dma((nb,)),
            dma((nb,)),
        ],
        compiler_params=pltpu.CompilerParams(
            collective_id=0, has_side_effects=True, vmem_limit_bytes=48 * 1024 * 1024
        ),
    )(*args)


def solution(mesh):
    dev = ("box", "sub")
    in_specs = (
        P(dev, None, None),
        P(dev, None),
        P(dev, None),
        P(dev, None, None),
        P(dev, None, None),
        P(dev, None, None),
        P(dev, None, None),
        P(),
        P("sub", None, None, None),
        P("sub", None, None, None),
        P(),
    )
    return jax.shard_map(
        functools.partial(local, mesh.shape["box"], mesh.shape["sub"]),
        mesh=mesh,
        in_specs=in_specs,
        out_specs=P(dev, None, None),
        check_vma=False,
    )
```

time: 82.8 us -> 25.9 us (0.31)
  blocking collectives: 41.5 us -> 0 us
  other arithmetic: 17.8 us -> 0 us
  Pallas kernels: 0 us -> 14.8 us
  starting transfers between devices: 7.25 us -> 0 us
  matrix products: 3.96 us -> 0 us
  local copies, waits for them, and re-layouts: 11.8 us -> 10.7 us
    all_gather x1 -> x0, blocking collectives: 30.8 us -> none  [local(): lax.all_gather(top_sum[None], 'box', axis=0, tiled=True)]
    pallas_call x0 -> x1, Pallas kernels: none -> 14.8 us  [local(): pl.pallas_call(functools.partial(kernel, nb, ns), out_shape=jax.ShapeDtyp...]
    scatter-add x1 -> x0, other arithmetic: 10.7 us -> none  [local(): jax.ops.segment_sum(stacked * weights[:, None], segment_ids, num_segments...]
    psum x1 -> x0, blocking collectives: 10.7 us -> none  [local(): top_sum = lax.psum(partial_value, 'sub')]
    all_to_all x1 -> x0, starting transfers between devices: 7.25 us -> none  [local(): lax.all_to_all(outgoing, 'box', split_axis=0, concat_axis=0, tiled=True)]
    gather x2 -> x0, local copies, waits for them, and re-layouts: 5.22 us -> none  [the longest x1 3.06 us: local(): near_rows = leaves[local_src]]
    unnamed x10 -> x17, local copies, waits for them, and re-layouts: 5.83 us -> 10.7 us
    convert_element_type x2 -> x0, other arithmetic: 3.99 us -> none  [the longest x1 3.22 us: local(): summed.astype(jnp.bfloat16)]
  transfers between devices with their start and end apart: 1 -> 0, of which waited for: 0 -> 0; matrix products, arithmetic and copies ran while one was open for 16% -> 0% of each run, Pallas kernels for 0% -> 0%
where the time goes in v1:
time: 25.9 us; the launch traced here: 25.5 us
  Pallas kernels  14.8 us (57%)
  local copies, waits for them, and re-layouts  10.7 us (41%)
    pallas_call x1, Pallas kernels, local(): pl.pallas_call(functools.partial(kernel, nb, ns), out_shape=jax.ShapeDtyp...  14.8 us
    unnamed x17, local copies, waits for them, and re-layouts  10.7 us

profile of v1, /device:TPU:0, one launch (start us, length us, event | category | flops | bytes accessed | tf_op | source)
XLA Modules:
  0.0 25.5 jit_solution(5923259992680099273)
XLA Ops:
  0.0 0.8 %copy.14.send_box = s32[1,8,2]{2,1,0:T(8,128)S(1)} copy(s32[1,8,2]{1,2,0:T(2,128)} %param.14) | data formatting | bytes 128 | tf_op args[3]
  0.8 0.8 %copy.15.recv_tgt = s32[1,8,2]{2,1,0:T(8,128)S(1)} copy(s32[1,8,2]{1,2,0:T(2,128)} %param.15) | data formatting | bytes 128 | tf_op args[4]
  1.5 0.8 %copy.16.recv_cls = s32[1,8,2]{2,1,0:T(8,128)S(1)} copy(s32[1,8,2]{1,2,0:T(2,128)} %param.16) | data formatting | bytes 128 | tf_op args[5]
  2.3 0.8 %copy.17.recv_live = s32[1,8,2]{2,1,0:T(8,128)S(1)} copy(s32[1,8,2]{1,2,0:T(2,128)} %param.17) | data formatting | bytes 128 | tf_op args[6]
  3.0 0.8 %copy.12.src_ref = s32[32,8]{1,0:T(8,128)S(1)} copy(s32[32,8]{0,1:T(8,128)} %param.12) | data formatting | bytes 2048 | tf_op args[1]
  3.8 0.8 %copy.13.cls_ref = s32[32,8]{1,0:T(8,128)S(1)} copy(s32[32,8]{0,1:T(8,128)} %param.13) | data formatting | bytes 2048 | tf_op args[2]
  4.5 0.0 copy-start
  4.5 1.4 %copy-done = bf16[12,256,256]{2,1,0:T(8,128)(2,1)S(1)} copy-done((bf16[12,256,256]{2,1,0:T(8,128)(2,1)S(1)}, bf16[12,256,256]{2,1,0:T(8,128)(2,1)}, u32[]{:S(2)}) %copy-start) | copy-done | bytes 1572888
  5.9 0.0 copy-start.1
  5.9 1.2 %copy-done.1 = bf16[1,8,256,256]{3,2,1,0:T(8,128)(2,1)S(1)} copy-done((bf16[1,8,256,256]{3,2,1,0:T(8,128)(2,1)S(1)}, bf16[1,8,256,256]{3,2,1,0:T(8,128)(2,1)}, u32[]{:S(2)}) %copy-start.1) | copy-done | bytes 1048600
  7.2 0.0 copy-start.2
  7.2 1.2 %copy-done.2 = bf16[1,8,256,256]{3,2,1,0:T(8,128)(2,1)S(1)} copy-done((bf16[1,8,256,256]{3,2,1,0:T(8,128)(2,1)S(1)}, bf16[1,8,256,256]{3,2,1,0:T(8,128)(2,1)}, u32[]{:S(2)}) %copy-start.2) | copy-done | bytes 1048600
  8.4 0.0 copy-start.3
  8.4 0.9 %copy-done.3 = bf16[32,16,256]{2,1,0:T(8,128)(2,1)S(1)} copy-done((bf16[32,16,256]{2,1,0:T(8,128)(2,1)S(1)}, bf16[32,16,256]{2,1,0:T(8,128)(2,1)}, u32[]{:S(2)}) %copy-start.3) | copy-done | bytes 262168
  9.3 0.0 copy-start.4
  9.3 0.7 %copy-done.4 = f32[8,8]{1,0:T(8,128)S(1)} copy-done((f32[8,8]{1,0:T(8,128)S(1)}, f32[8,8]{1,0:T(8,128)}, u32[]{:S(2)}) %copy-start.4) | copy-done | bytes 280
  10.0 14.8 %shard_map.109 = bf16[32,16,256]{2,1,0:T(8,128)(2,1)S(1)} custom-call(bf16[32,16,256]{2,1,0:T(8,128)(2,1)S(1)} %copy-done.3, s32[32,8]{1,0:T(8,128)S(1)} %copy.12.src_ref, s32[32,8]{1,0:T(8,128)S(1)} %copy.13.cls_ref, s32[1,8,2]{2,1,0:T(8,128)S(1)} %copy.14.send_box, s32[1,8,2]{2,1,0:T(8,128)S(1)} %copy.15.recv_tgt, s32[1,8,2]{2,1,0:T(8,128)S(1)} %copy.16.recv_cls, ...), custom_call_target="tpu_custom_call" | custom-call | tf_op jit(solution)/shard_map/pallas_call | solution.py:270
  24.8 0.7 %copy.19 = bf16[32,16,256]{2,1,0:T(8,128)(2,1)} copy(bf16[32,16,256]{2,1,0:T(8,128)(2,1)S(1)} %shard_map.109) | data formatting | bytes 524288
Async XLA Ops:
  4.5 1.4 %copy-start = (bf16[12,256,256]{2,1,0:T(8,128)(2,1)S(1)}, bf16[12,256,256]{2,1,0:T(8,128)(2,1)}, u32[]{:S(2)}) copy-start(bf16[12,256,256]{2,1,0:T(8,128)(2,1)} %trans_hbm.1) | copy-start | bytes 4718596
  5.9 1.2 %copy-start.1 = (bf16[1,8,256,256]{3,2,1,0:T(8,128)(2,1)S(1)}, bf16[1,8,256,256]{3,2,1,0:T(8,128)(2,1)}, u32[]{:S(2)}) copy-start(bf16[1,8,256,256]{3,2,1,0:T(8,128)(2,1)} %up_hbm.1) | copy-start | bytes 3145732
  7.2 1.2 %copy-start.2 = (bf16[1,8,256,256]{3,2,1,0:T(8,128)(2,1)S(1)}, bf16[1,8,256,256]{3,2,1,0:T(8,128)(2,1)}, u32[]{:S(2)}) copy-start(bf16[1,8,256,256]{3,2,1,0:T(8,128)(2,1)} %down_hbm.1) | copy-start | bytes 3145732
  8.4 0.9 %copy-start.3 = (bf16[32,16,256]{2,1,0:T(8,128)(2,1)S(1)}, bf16[32,16,256]{2,1,0:T(8,128)(2,1)}, u32[]{:S(2)}) copy-start(bf16[32,16,256]{2,1,0:T(8,128)(2,1)} %leaves_hbm.1) | copy-start | bytes 786436
  9.3 0.7 %copy-start.4 = (f32[8,8]{1,0:T(8,128)S(1)}, f32[8,8]{1,0:T(8,128)}, u32[]{:S(2)}) copy-start(f32[8,8]{1,0:T(8,128)} %coupling.1) | copy-start | bytes 772

commit v2 on v1

--- a/solution.py
+++ b/solution.py
@@ -28,17 +28,24 @@
     nb,
     ns,
     leaves_hbm,
+    src_hbm,
+    cls_hbm,
+    send_hbm,
+    tgt_hbm,
+    rcls_hbm,
+    live_hbm,
+    trans_hbm,
+    up_hbm,
+    down_hbm,
+    coupling_hbm,
+    out_ref,
     src_ref,
     cls_ref,
     send_box,
     recv_tgt,
     recv_cls,
     recv_live,
-    trans_hbm,
-    up_hbm,
-    down_hbm,
     coupling,
-    out_ref,
     leaves,
     trans,
     up,
@@ -53,6 +60,9 @@
     counts,
     grouped,
     near,
+    swap_in,
+    swap_slots,
+    swap_back,
     load_sem,
     slot_send,
     slot_recv,
@@ -87,65 +97,50 @@
     over(ns, lambda d: pl.semaphore_signal(barrier, inc=1, device_id=sub_peer(d), device_id_type=MESH))
     over(nb, lambda d: pl.semaphore_signal(barrier, inc=1, device_id=box_peer(d), device_id_type=MESH))
 
-    loads = [
-        pltpu.make_async_copy(leaves_hbm, leaves, load_sem.at[0]),
-        pltpu.make_async_copy(up_hbm.at[0], up, load_sem.at[1]),
-        pltpu.make_async_copy(trans_hbm, trans, load_sem.at[2]),
-        pltpu.make_async_copy(down_hbm.at[0], down, load_sem.at[3]),
-    ]
+    pairs = (
+        (leaves_hbm, leaves),
+        (send_hbm, send_box),
+        (up_hbm.at[0], up),
+        (src_hbm, src_ref),
+        (cls_hbm, cls_ref),
+        (tgt_hbm, recv_tgt),
+        (rcls_hbm, recv_cls),
+        (live_hbm, recv_live),
+        (coupling_hbm, coupling),
+        (trans_hbm, trans),
+        (down_hbm.at[0], down),
+    )
+    loads = [pltpu.make_async_copy(a, b, load_sem.at[n]) for n, (a, b) in enumerate(pairs)]
     for load in loads:
         load.start()
 
-    lane = lax.broadcasted_iota(jnp.int32, (1, depth), 1)
-    slot_code = jnp.full((1, depth), -1, jnp.int32)
-
-    def add_slot(d, c, code):
-        k = lax.rem(box - d + nb, nb)
-        value = recv_cls[0, k, c] * boxes + recv_tgt[0, k, c]
-        value = jnp.where(recv_live[0, k, c] != 0, value, -1)
-        return jnp.where(lane == boxes + d * cap + c, value, code)
-
-    if nb <= 16:
-        for d in range(nb):
-            for c in range(cap):
-                slot_code = add_slot(d, c, slot_code)
-    else:
-        def add_peer(d, code):
-            for c in range(cap):
-                code = add_slot(d, c, code)
-            return code
-
-        slot_code = lax.fori_loop(0, nb, add_peer, slot_code)
-    own_code = cls_ref[...] * depth + src_ref[...]
-    target = lax.broadcasted_iota(jnp.int32, (boxes, depth), 0)
-    for q in range(classes):
-        total = jnp.where(slot_code == q * boxes + target, 1.0, 0.0)
-        for n in range(own_code.shape[1]):
-            total += jnp.where(own_code[:, n : n + 1] == q * depth + lane, 1.0, 0.0)
-        counts[q * boxes : (q + 1) * boxes, :] = total.astype(BF16)
+    group = 16
+    swap_in[...] = swap_matrix(rhs, boxes)
+    swap_slots[...] = swap_matrix(rhs, group)
+    swap_back[...] = swap_matrix(boxes, rhs)
 
     loads[0].wait()
-
-    if nb <= 16:
-        for d in range(nb):
-            for c in range(cap):
-                k = lax.rem(box + d, nb)
-                outgoing[d, c] = leaves[send_box[0, k, c]]
-    else:
-        @pl.loop(0, nb)
-        def _(d):
-            for c in range(cap):
-                outgoing[d, c] = leaves[send_box[0, lax.rem(box + d, nb), c]]
-
-    for c in range(cap):
-        arrived[0, c] = outgoing[0, c]
-
     child = leaves[0:children].astype(F32)
     for g in range(1, boxes // children):
         child += leaves[g * children : (g + 1) * children].astype(F32)
     child = child.astype(BF16)
 
     loads[1].wait()
+    if nb <= 16:
+        for d in range(nb):
+            for c in range(cap):
+                outgoing[d, c] = leaves[send_box[0, c, lax.rem(box + d, nb)]]
+    else:
+
+        @pl.loop(0, nb)
+        def _(d):
+            for c in range(cap):
+                outgoing[d, c] = leaves[send_box[0, c, lax.rem(box + d, nb)]]
+
+    for c in range(cap):
+        arrived[0, c] = outgoing[0, c]
+
+    loads[2].wait()
     part = dot_nt(child[0], up[0])
     for m in range(1, children):
         part += dot_nt(child[m], up[m])
@@ -188,7 +183,7 @@
 
     mixed[:, 0:boxes, :] = (
         jnp.dot(
-            swap_matrix(rhs, boxes),
+            swap_in[...],
             leaves[...].reshape(boxes * rhs, width),
             preferred_element_type=F32,
         )
@@ -203,14 +198,42 @@
     top_out[...] = top.astype(BF16)
     over(nb, lambda d: top_copy(d).start())
 
+
+    for load in loads[3:9]:
+        load.wait()
+    lane = lax.broadcasted_iota(jnp.int32, (1, depth), 1)
+
+    def add_slot(d, c, code):
+        k = lax.rem(box - d + nb, nb)
+        value = recv_cls[0, c, k] * boxes + recv_tgt[0, c, k]
+        value = jnp.where(recv_live[0, c, k] != 0, value, -1)
+        return jnp.where(lane == boxes + d * cap + c, value, code)
+
+    def add_peer(d, code):
+        for c in range(cap):
+            code = add_slot(d, c, code)
+        return code
+
+    slot_code = jnp.full((1, depth), -1, jnp.int32)
+    if nb <= 16:
+        for d in range(nb):
+            slot_code = add_peer(d, slot_code)
+    else:
+        slot_code = lax.fori_loop(0, nb, add_peer, slot_code)
+    own_code = jnp.transpose(cls_ref[...] * depth + src_ref[...])
+    target = lax.broadcasted_iota(jnp.int32, (boxes, depth), 0)
+    for q in range(classes):
+        total = jnp.where(slot_code == q * boxes + target, 1.0, 0.0)
+        for n in range(own_code.shape[1]):
+            total += jnp.where(own_code[:, n : n + 1] == q * depth + lane, 1.0, 0.0)
+        counts[q * boxes : (q + 1) * boxes, :] = total.astype(BF16)
+
     over(nb, lambda d: slot_copy(d).wait_recv())
-    group = 16
-    swap_slots = swap_matrix(rhs, group)
     per_group = group // cap
     for g in range(slots // group):
         rows = arrived[g * per_group : (g + 1) * per_group].reshape(group * rhs, width)
         mixed[:, boxes + g * group : boxes + (g + 1) * group, :] = (
-            jnp.dot(swap_slots, rows, preferred_element_type=F32)
+            jnp.dot(swap_slots[...], rows, preferred_element_type=F32)
             .astype(BF16)
             .reshape(rhs, group, width)
         )
@@ -219,19 +242,18 @@
         held = jnp.dot(counts[...], mixed[s], preferred_element_type=F32).astype(BF16)
         grouped[:, s * boxes : (s + 1) * boxes, :] = held.reshape(classes, boxes, width)
 
-    loads[2].wait()
+    loads[9].wait()
     total = dot_nt(grouped[0], trans[0])
     for q in range(1, classes):
         total += dot_nt(grouped[q], trans[q])
     high = total.astype(BF16)
     low = (total - high.astype(F32)).astype(BF16)
-    back = swap_matrix(boxes, rhs)
     near[...] = (
-        jnp.dot(back, high, preferred_element_type=F32)
-        + jnp.dot(back, low, preferred_element_type=F32)
+        jnp.dot(swap_back[...], high, preferred_element_type=F32)
+        + jnp.dot(swap_back[...], low, preferred_element_type=F32)
     ).reshape(boxes, rhs, width)
 
-    loads[3].wait()
+    loads[10].wait()
     over(nb, lambda d: top_copy(d).wait_recv())
     far = coupling[box, box] * top
     if nb <= 16:
@@ -263,16 +285,25 @@
     cap = send_box.shape[2]
     classes = translation.shape[0]
     depth = boxes + nb * cap
+    rows = boxes * rhs
     vmem = pl.BlockSpec(memory_space=pltpu.VMEM)
-    smem = pl.BlockSpec(memory_space=pltpu.SMEM)
-    hbm = pl.BlockSpec(memory_space=pl.ANY)
+    hbm = pl.BlockSpec(memory_space=pltpu.HBM)
     dma = pltpu.SemaphoreType.DMA
+    int_vmem = pltpu.VMEM(local_src.shape[::-1], jnp.int32)
+    int_smem = pltpu.SMEM((1, cap, nb), jnp.int32)
     return pl.pallas_call(
         functools.partial(kernel, nb, ns),
         out_shape=jax.ShapeDtypeStruct(leaves.shape, BF16),
-        in_specs=[hbm, vmem, vmem, smem, smem, smem, smem, hbm, hbm, hbm, smem],
+        in_specs=[hbm] * 11,
         out_specs=vmem,
         scratch_shapes=[
+            int_vmem,
+            int_vmem,
+            int_smem,
+            int_smem,
+            int_smem,
+            int_smem,
+            pltpu.SMEM(coupling.shape, F32),
             pltpu.VMEM((boxes, rhs, width), BF16),
             pltpu.VMEM(translation.shape, BF16),
             pltpu.VMEM(up_maps.shape[1:], BF16),
@@ -287,7 +318,10 @@
             pltpu.VMEM((classes * boxes, depth), BF16),
             pltpu.VMEM((classes, rhs * boxes, width), BF16),
             pltpu.VMEM((boxes, rhs, width), F32),
-            dma((4,)),
+            pltpu.VMEM((rows, rows), BF16),
+            pltpu.VMEM((16 * rhs, 16 * rhs), BF16),
+            pltpu.VMEM((rows, rows), BF16),
+            dma((11,)),
             dma((nb,)),
             dma((nb,)),
             dma((ns,)),
@@ -296,9 +330,18 @@
             dma((nb,)),
         ],
         compiler_params=pltpu.CompilerParams(
-            collective_id=0, has_side_effects=True, vmem_limit_bytes=48 * 1024 * 1024
+            collective_id=0, has_side_effects=True, vmem_limit_bytes=64 * 1024 * 1024
         ),
-    )(*args)
+    )(
+        leaves,
+        local_src.T,
+        local_cls.T,
+        *(jnp.transpose(a, (0, 2, 1)) for a in (send_box, recv_tgt, recv_cls, recv_live)),
+        translation,
+        up_maps,
+        down_maps,
+        coupling,
+    )
 
 
 def solution(mesh):

time: 25.9 us -> 16.9 us (0.65)
  local copies, waits for them, and re-layouts: 10.7 us -> 1.67 us
    unnamed x17 -> x1, local copies, waits for them, and re-layouts: 10.7 us -> 1.67 us
    pallas_call x1, Pallas kernels: 14.8 us -> 15 us  [local(): pl.pallas_call(functools.partial(kernel, nb, ns), out_shape=jax.ShapeDtyp...]
where the time goes in v2:
time: 16.9 us; the launch traced here: 16.7 us
  Pallas kernels  15 us (89%)
  local copies, waits for them, and re-layouts  1.67 us (10%)
    pallas_call x1, Pallas kernels, local(): pl.pallas_call(functools.partial(kernel, nb, ns), out_shape=jax.ShapeDtyp...  15 us
    unnamed x1, local copies, waits for them, and re-layouts  1.67 us

profile of v2, /device:TPU:0, one launch (start us, length us, event | category | flops | bytes accessed | tf_op | source)
XLA Modules:
  0.0 16.7 jit_solution(2241074755654572115)
XLA Ops:
  0.0 15.0 %shard_map.109 = bf16[32,16,256]{2,1,0:T(8,128)(2,1)} custom-call(bf16[32,16,256]{2,1,0:T(8,128)(2,1)} %leaves_hbm.1, s32[8,32]{1,0:T(8,128)} %bitcast.6, s32[8,32]{1,0:T(8,128)} %bitcast.7, s32[1,2,8]{2,1,0:T(2,128)} %bitcast.8, s32[1,2,8]{2,1,0:T(2,128)} %bitcast.9, s32[1,2,8]{2,1,0:T(2,128)} %bitcast.10, s32[1,2,8]{2,1,0:T(2,128)} %bitcast.11, ...), custom_call_target="tpu_custom_call" | custom-call | tf_op jit(solution)/shard_map/pallas_call | solution.py:294
  15.0 1.7 %copy.13 = bf16[32,16,256]{2,1,0:T(8,128)(2,1)} copy(bf16[32,16,256]{2,1,0:T(8,128)(2,1)} %shard_map.109) | data formatting | bytes 524288

commit v3 on v2

--- a/solution.py
+++ b/solution.py
@@ -291,6 +291,16 @@
     dma = pltpu.SemaphoreType.DMA
     int_vmem = pltpu.VMEM(local_src.shape[::-1], jnp.int32)
     int_smem = pltpu.SMEM((1, cap, nb), jnp.int32)
+    operands = (
+        leaves,
+        local_src.T,
+        local_cls.T,
+        *(jnp.transpose(a, (0, 2, 1)) for a in (send_box, recv_tgt, recv_cls, recv_live)),
+        translation,
+        up_maps,
+        down_maps,
+        coupling,
+    )
     return pl.pallas_call(
         functools.partial(kernel, nb, ns),
         out_shape=jax.ShapeDtypeStruct(leaves.shape, BF16),
@@ -330,18 +340,9 @@
             dma((nb,)),
         ],
         compiler_params=pltpu.CompilerParams(
-            collective_id=0, has_side_effects=True, vmem_limit_bytes=64 * 1024 * 1024
+            collective_id=0, has_side_effects=True, vmem_limit_bytes=48 * 1024 * 1024
         ),
-    )(
-        leaves,
-        local_src.T,
-        local_cls.T,
-        *(jnp.transpose(a, (0, 2, 1)) for a in (send_box, recv_tgt, recv_cls, recv_live)),
-        translation,
-        up_maps,
-        down_maps,
-        coupling,
-    )
+    )(*(pltpu.with_memory_space_constraint(a, pltpu.HBM) for a in operands))
 
 
 def solution(mesh):

time: 16.9 us -> 15.2 us (0.90)
  local copies, waits for them, and re-layouts: 1.67 us -> 0.71 us
  Pallas kernels: 15 us -> 14.3 us
    unnamed x1, local copies, waits for them, and re-layouts: 1.67 us -> 0.71 us
    pallas_call x1, Pallas kernels: 15 us -> 14.3 us  [local(): pl.pallas_call(functools.partial(kernel, nb, ns), out_shape=jax.ShapeDtyp...]
where the time goes in v3:
time: 15.2 us; the launch traced here: 15.1 us
  Pallas kernels  14.3 us (94%)
  local copies, waits for them, and re-layouts  0.71 us (5%)
    pallas_call x1, Pallas kernels, local(): pl.pallas_call(functools.partial(kernel, nb, ns), out_shape=jax.ShapeDtyp...  14.3 us
    unnamed x1, local copies, waits for them, and re-layouts  0.71 us

profile of v3, /device:TPU:0, one launch (start us, length us, event | category | flops | bytes accessed | tf_op | source)
XLA Modules:
  0.0 15.1 jit_solution(9022918776177570902)
XLA Ops:
  0.0 14.3 %shard_map.109 = bf16[32,16,256]{2,1,0:T(8,128)(2,1)S(1)} custom-call(bf16[32,16,256]{2,1,0:T(8,128)(2,1)} %leaves_hbm.1, s32[8,32]{1,0:T(8,128)} %bitcast.6, s32[8,32]{1,0:T(8,128)} %bitcast.7, s32[1,2,8]{2,1,0:T(2,128)} %bitcast.8, s32[1,2,8]{2,1,0:T(2,128)} %bitcast.9, s32[1,2,8]{2,1,0:T(2,128)} %bitcast.10, s32[1,2,8]{2,1,0:T(2,128)} %bitcast.11, ...), custom_call_target="tpu_custom_call" | custom-call | tf_op jit(solution)/shard_map/pallas_call | solution.py:304
  14.3 0.7 %copy.13 = bf16[32,16,256]{2,1,0:T(8,128)(2,1)} copy(bf16[32,16,256]{2,1,0:T(8,128)(2,1)S(1)} %shard_map.109) | data formatting | bytes 524288

commit v4 on v3

--- a/solution.py
+++ b/solution.py
@@ -61,7 +61,8 @@
     grouped,
     near,
     swap_in,
-    swap_slots,
+    row_cls,
+    spread,
     swap_back,
     load_sem,
     slot_send,
@@ -78,7 +79,8 @@
     classes = trans.shape[0]
     children = up.shape[0]
     slots = nb * cap
-    depth = boxes + slots
+    group = 16
+    rows = group * rhs
 
     def box_peer(d):
         return (lax.rem(box + d, nb), sub)
@@ -111,20 +113,15 @@
         (down_hbm.at[0], down),
     )
     loads = [pltpu.make_async_copy(a, b, load_sem.at[n]) for n, (a, b) in enumerate(pairs)]
-    for load in loads:
+    for load in loads[:9]:
         load.start()
 
-    group = 16
     swap_in[...] = swap_matrix(rhs, boxes)
-    swap_slots[...] = swap_matrix(rhs, group)
     swap_back[...] = swap_matrix(boxes, rhs)
 
     loads[0].wait()
-    child = leaves[0:children].astype(F32)
-    for g in range(1, boxes // children):
-        child += leaves[g * children : (g + 1) * children].astype(F32)
-    child = child.astype(BF16)
-
+    for load in loads[9:]:
+        load.start()
     loads[1].wait()
     if nb <= 16:
         for d in range(nb):
@@ -139,12 +136,6 @@
 
     for c in range(cap):
         arrived[0, c] = outgoing[0, c]
-
-    loads[2].wait()
-    part = dot_nt(child[0], up[0])
-    for m in range(1, children):
-        part += dot_nt(child[m], up[m])
-    part_out[...] = part.astype(BF16)
 
     pl.semaphore_wait(barrier, nb + ns - 2)
 
@@ -178,10 +169,32 @@
             device_id_type=MESH,
         )
 
+    over(nb, lambda d: slot_copy(d).start())
+
+    child = leaves[0:children].astype(F32)
+    for g in range(1, boxes // children):
+        child += leaves[g * children : (g + 1) * children].astype(F32)
+    child = child.astype(BF16)
+
+    loads[2].wait()
+    part = dot_nt(child[0], up[0])
+    for m in range(1, children):
+        part += dot_nt(child[m], up[m])
+    part_out[...] = part.astype(BF16)
     over(ns, lambda d: part_copy(d).start())
-    over(nb, lambda d: slot_copy(d).start())
-
-    mixed[:, 0:boxes, :] = (
+
+    for load in loads[3:9]:
+        load.wait()
+
+    lane = lax.broadcasted_iota(jnp.int32, (1, boxes), 1)
+    own_code = jnp.transpose(cls_ref[...] * boxes + src_ref[...])
+    for q in range(classes):
+        total = jnp.zeros((boxes, boxes), F32)
+        for n in range(own_code.shape[1]):
+            total += jnp.where(own_code[:, n : n + 1] == q * boxes + lane, 1.0, 0.0)
+        counts[q * boxes : (q + 1) * boxes, :] = total.astype(BF16)
+
+    mixed[...] = (
         jnp.dot(
             swap_in[...],
             leaves[...].reshape(boxes * rhs, width),
@@ -190,6 +203,9 @@
         .astype(BF16)
         .reshape(rhs, boxes, width)
     )
+    for s in range(rhs):
+        held = jnp.dot(counts[...], mixed[s], preferred_element_type=F32).astype(BF16)
+        grouped[:, s * boxes : (s + 1) * boxes, :] = held.reshape(classes, boxes, width)
 
     top = part
     over(ns, lambda d: part_copy(d).wait_recv())
@@ -199,48 +215,26 @@
     over(nb, lambda d: top_copy(d).start())
 
 
-    for load in loads[3:9]:
-        load.wait()
-    lane = lax.broadcasted_iota(jnp.int32, (1, depth), 1)
-
-    def add_slot(d, c, code):
+    across = lax.broadcasted_iota(jnp.int32, (1, slots * rhs), 1)
+
+    def place(d, goal):
         k = lax.rem(box - d + nb, nb)
-        value = recv_cls[0, c, k] * boxes + recv_tgt[0, c, k]
-        value = jnp.where(recv_live[0, c, k] != 0, value, -1)
-        return jnp.where(lane == boxes + d * cap + c, value, code)
-
-    def add_peer(d, code):
         for c in range(cap):
-            code = add_slot(d, c, code)
-        return code
-
-    slot_code = jnp.full((1, depth), -1, jnp.int32)
+            first = (d * cap + c) * rhs
+            row_cls[pl.ds(first, rhs), :] = jnp.full((rhs, width), recv_cls[0, c, k], jnp.int32)
+            aim = jnp.where(recv_live[0, c, k] != 0, recv_tgt[0, c, k] * rhs, -slots * rhs) - first
+            inside = (across >= first) & (across < first + rhs)
+            goal = jnp.where(inside, across + aim, goal)
+        return goal
+
+    goal = jnp.full((1, slots * rhs), -1, jnp.int32)
     if nb <= 16:
         for d in range(nb):
-            slot_code = add_peer(d, slot_code)
+            goal = place(d, goal)
     else:
-        slot_code = lax.fori_loop(0, nb, add_peer, slot_code)
-    own_code = jnp.transpose(cls_ref[...] * depth + src_ref[...])
-    target = lax.broadcasted_iota(jnp.int32, (boxes, depth), 0)
-    for q in range(classes):
-        total = jnp.where(slot_code == q * boxes + target, 1.0, 0.0)
-        for n in range(own_code.shape[1]):
-            total += jnp.where(own_code[:, n : n + 1] == q * depth + lane, 1.0, 0.0)
-        counts[q * boxes : (q + 1) * boxes, :] = total.astype(BF16)
-
-    over(nb, lambda d: slot_copy(d).wait_recv())
-    per_group = group // cap
-    for g in range(slots // group):
-        rows = arrived[g * per_group : (g + 1) * per_group].reshape(group * rhs, width)
-        mixed[:, boxes + g * group : boxes + (g + 1) * group, :] = (
-            jnp.dot(swap_slots[...], rows, preferred_element_type=F32)
-            .astype(BF16)
-            .reshape(rhs, group, width)
-        )
-
-    for s in range(rhs):
-        held = jnp.dot(counts[...], mixed[s], preferred_element_type=F32).astype(BF16)
-        grouped[:, s * boxes : (s + 1) * boxes, :] = held.reshape(classes, boxes, width)
+        goal = lax.fori_loop(0, nb, place, goal)
+    target = lax.broadcasted_iota(jnp.int32, (boxes * rhs, slots * rhs), 0)
+    spread[...] = jnp.where(target == goal, 1.0, 0.0).astype(BF16)
 
     loads[9].wait()
     total = dot_nt(grouped[0], trans[0])
@@ -252,6 +246,17 @@
         jnp.dot(swap_back[...], high, preferred_element_type=F32)
         + jnp.dot(swap_back[...], low, preferred_element_type=F32)
     ).reshape(boxes, rhs, width)
+
+    over(nb, lambda d: slot_copy(d).wait_recv())
+    for g in range(slots // group):
+        some = arrived[g * group // cap : (g + 1) * group // cap].reshape(rows, width)
+        which = row_cls[g * rows : (g + 1) * rows, :]
+        moved = dot_nt(some, trans[0])
+        for q in range(1, classes):
+            moved = jnp.where(which == q, dot_nt(some, trans[q]), moved)
+        near[...] += jnp.dot(
+            spread[:, g * rows : (g + 1) * rows], moved.astype(BF16), preferred_element_type=F32
+        ).reshape(boxes, rhs, width)
 
     loads[10].wait()
     over(nb, lambda d: top_copy(d).wait_recv())
@@ -284,7 +289,6 @@
     boxes, rhs, width = leaves.shape
     cap = send_box.shape[2]
     classes = translation.shape[0]
-    depth = boxes + nb * cap
     rows = boxes * rhs
     vmem = pl.BlockSpec(memory_space=pltpu.VMEM)
     hbm = pl.BlockSpec(memory_space=pltpu.HBM)
@@ -324,12 +328,13 @@
             pltpu.VMEM((ns, rhs, width), BF16),
             pltpu.VMEM((rhs, width), BF16),
             pltpu.VMEM((nb, rhs, width), BF16),
-            pltpu.VMEM((rhs, depth, width), BF16),
-            pltpu.VMEM((classes * boxes, depth), BF16),
+            pltpu.VMEM((rhs, boxes, width), BF16),
+            pltpu.VMEM((classes * boxes, boxes), BF16),
             pltpu.VMEM((classes, rhs * boxes, width), BF16),
             pltpu.VMEM((boxes, rhs, width), F32),
             pltpu.VMEM((rows, rows), BF16),
-            pltpu.VMEM((16 * rhs, 16 * rhs), BF16),
+            pltpu.VMEM((nb * cap * rhs, width), jnp.int32),
+            pltpu.VMEM((rows, nb * cap * rhs), BF16),
             pltpu.VMEM((rows, rows), BF16),
             dma((11,)),
             dma((nb,)),

time: 15.2 us -> 15.3 us (level)
  no operation moved by 1% of the time
where the time goes in v4:
time: 15.3 us; the launch traced here: 15.2 us
  Pallas kernels  14.4 us (94%)
  local copies, waits for them, and re-layouts  0.71 us (5%)
    pallas_call x1, Pallas kernels, local(): pl.pallas_call(functools.partial(kernel, nb, ns), out_shape=jax.ShapeDtyp...  14.4 us
    unnamed x1, local copies, waits for them, and re-layouts  0.71 us

profile of v4, /device:TPU:0, one launch (start us, length us, event | category | flops | bytes accessed | tf_op | source)
XLA Modules:
  0.0 15.2 jit_solution(14011227845785446806)
XLA Ops:
  0.0 14.4 %shard_map.109 = bf16[32,16,256]{2,1,0:T(8,128)(2,1)S(1)} custom-call(bf16[32,16,256]{2,1,0:T(8,128)(2,1)} %leaves_hbm.1, s32[8,32]{1,0:T(8,128)} %bitcast.6, s32[8,32]{1,0:T(8,128)} %bitcast.7, s32[1,2,8]{2,1,0:T(2,128)} %bitcast.8, s32[1,2,8]{2,1,0:T(2,128)} %bitcast.9, s32[1,2,8]{2,1,0:T(2,128)} %bitcast.10, s32[1,2,8]{2,1,0:T(2,128)} %bitcast.11, ...), custom_call_target="tpu_custom_call" | custom-call | tf_op jit(solution)/shard_map/pallas_call | solution.py:308
  14.4 0.7 %copy.13 = bf16[32,16,256]{2,1,0:T(8,128)(2,1)} copy(bf16[32,16,256]{2,1,0:T(8,128)(2,1)S(1)} %shard_map.109) | data formatting | bytes 524288
